TPU v7x, 32 devices: a whole 2x2x4 slice. The times are simulated.
32 devices in a mesh: dp: 16 (over z, y, x), block: 2 (over core).
Axes of the slice: x: 2, y: 2, z: 4, core: 2. Of those that a mesh axis runs over, the one named last changes fastest.
Arguments:
- tokens: bfloat16 [16, 256, 4096], P('dp', 'block'), may hold values from -6 to 6
- cotangent: bfloat16 [16, 256, 4096], P('dp', 'block'), may hold values from -6 to 6
- w_up: bfloat16 [2, 4096, 512], P('block'), may hold values from -0.09375 to 0.09375
- w_down: bfloat16 [2, 512, 4096], P('block'), may hold values from -0.25 to 0.25
- active: int32 [16, 2], replicated, may hold values from 0 to 1, as said below
- width: int32 [16], replicated, may hold values from 8 to 16
- counts: int32 [2], replicated, may hold values from 16 to 63
Outputs:
- mixed: bfloat16 [16, 256, 4096], P('dp', 'block')
- input_grad: bfloat16 [16, 256, 4096], P('dp', 'block')
- up_grad: float32 [2, 4096, 512], P('block', 'dp')
- down_grad: float32 [2, 512, 4096], P('block', None, 'dp')
Inputs may be any that keep to these rules, and one draw needn't show every extreme that they name: `active`: 0 or 1; blocks differ in how many micro-batches use them. micro-batch i uses the first 256 * width[i] features.
All inputs are finite; a program needn't handle non-finite values.
Results may differ from a plain program's by a relative error of at most 0.019.
Values may be sent and summed in bfloat16 or wider, within the bound.
A program may use at most 128 MiB of HBM per device.

v0:
```python
import math

import jax
import jax.numpy as jnp
from jax import lax
from jax.sharding import PartitionSpec as P

GELU_C = math.sqrt(2.0 / math.pi)


def gelu_parts(pre_vals):
    tanh_val = jnp.tanh(GELU_C * (pre_vals + 0.044715 * pre_vals * pre_vals * pre_vals))
    gelu_value = 0.5 * pre_vals * (1.0 + tanh_val)
    gelu_slope = 0.5 * (1.0 + tanh_val) + 0.5 * pre_vals * (1.0 - tanh_val * tanh_val) * GELU_C * (
        1.0 + 3.0 * 0.044715 * pre_vals * pre_vals
    )
    return (gelu_value, gelu_slope)


def local(tokens, cotangent, w_up, w_down, active, width, counts):
    micro_index = lax.axis_index("dp")
    owner_index = lax.axis_index("block")
    local_count = w_up.shape[0]
    feats = tokens.shape[2]
    start_block = owner_index * local_count
    act_row = lax.dynamic_slice(active, (micro_index, start_block), (1, local_count))[0]
    gate_row = act_row.astype(jnp.float32)
    counts_here = lax.dynamic_slice(counts, (start_block,), (local_count,)).astype(jnp.float32)
    scale_row = gate_row / counts_here
    width_step = lax.dynamic_slice(width, (micro_index,), (1,))[0]
    width_limit = feats // 16 * width_step
    feat_mask = (lax.iota(jnp.int32, feats) < width_limit).astype(jnp.bfloat16)
    gathered = (
        lax.all_gather(tokens, "block", axis=1, tiled=True),
        lax.all_gather(cotangent, "block", axis=1, tiled=True),
    )
    whole_x = gathered[0][0]
    whole_dy = gathered[1][0]
    masked_x = whole_x * feat_mask
    masked_dy = whole_dy * feat_mask
    pre_act = jnp.einsum("rd,bdu->bru", masked_x, w_up, preferred_element_type=jnp.float32)
    gelu_value, gelu_slope = gelu_parts(pre_act)
    hidden = gelu_value.astype(jnp.bfloat16)
    products = jnp.einsum("bru,bud->brd", hidden, w_down, preferred_element_type=jnp.float32)
    mixed_sum = lax.psum_scatter(
        jnp.sum(products * gate_row[:, None, None], axis=0).astype(jnp.bfloat16),
        "block",
        scatter_dimension=0,
        tiled=True,
    ).astype(jnp.float32)
    down_term = scale_row[:, None, None] * jnp.einsum(
        "bru,rd->bud", hidden, masked_dy, preferred_element_type=jnp.float32
    )
    back_proj = jnp.einsum("rd,bud->bru", masked_dy, w_down, preferred_element_type=jnp.float32)
    grad_hidden = (back_proj * gelu_slope).astype(jnp.bfloat16)
    up_term = scale_row[:, None, None] * jnp.einsum(
        "rd,bru->bdu", masked_x, grad_hidden, preferred_element_type=jnp.float32
    )
    up_grad, down_grad = (
        lax.psum_scatter(
            up_term.astype(jnp.bfloat16), "dp", scatter_dimension=1, tiled=True
        ).astype(jnp.float32),
        lax.psum_scatter(
            down_term.astype(jnp.bfloat16), "dp", scatter_dimension=2, tiled=True
        ).astype(jnp.float32),
    )
    products = jnp.einsum("bru,bdu->brd", grad_hidden, w_up, preferred_element_type=jnp.float32)
    input_sum = lax.psum_scatter(
        jnp.sum(products * gate_row[:, None, None], axis=0).astype(jnp.bfloat16),
        "block",
        scatter_dimension=0,
        tiled=True,
    ).astype(jnp.float32)
    mask_float = feat_mask.astype(jnp.float32)
    mixed = (tokens[0].astype(jnp.float32) + mask_float * mixed_sum).astype(jnp.bfloat16)[None]
    input_grad = (cotangent[0].astype(jnp.float32) + mask_float * input_sum).astype(jnp.bfloat16)[
        None
    ]
    return (mixed, input_grad, up_grad, down_grad)


def solution(mesh):
    in_specs = (
        P("dp", "block", None),
        P("dp", "block", None),
        P("block", None, None),
        P("block", None, None),
        P(),
        P(),
        P(),
    )
    out_specs = (
        P("dp", "block", None),
        P("dp", "block", None),
        P("block", "dp", None),
        P("block", None, "dp"),
    )
    return jax.shard_map(local, mesh=mesh, in_specs=in_specs, out_specs=out_specs, check_vma=False)
```

profile of v0, /device:TPU:0, one launch (start us, length us, event | category | flops | bytes accessed | tf_op | source)
XLA Modules:
  0.0 266.3 jit_solution(7529655962990842818)
XLA Ops:
  7.2 0.7 all-gather.3.cloned.1.call-update
  8.0 0.7 all-gather.5.cloned.1.call-update
  8.7 0.6 dynamic_slice.9
  9.3 0.6 dynamic_slice.10
  11.2 11.7 %all-gather.3.cloned.1.call-done = bf16[1,256,4096]{2,1,0:T(8,128)(2,1)} async-done(((bf16[1,128,4096]{2,1,0:T(8,128)(2,1)}), bf16[1,256,4096]{2,1,0:T(8,128)(2,1)}) %all-gather.3.cloned.1.call-update) | async-done | bytes 2097168 | tf_op jit(solution)/shard_map/all_gather | solution.py:34
  22.9 4.2 %fusion.20 = f32[1,256,512]{2,1,0:T(8,128)S(1)} fusion(bf16[1,4096,512]{2,1,0:T(8,128)(2,1)} %param.9, bf16[1,256,4096]{2,1,0:T(8,128)(2,1)} %all-gather.3.cloned.1.call-done, bf16[4096]{0:T(1024)(128)(2,1)S(1)} %fusion.58), kind=kOutput, calls=%fused_computation.26 | convolution fusion | flops 1074790400 | bytes 6823936 | tf_op jit(solution)/shard_map/rd,bdu->bru/dot_general | solution.py:41
  27.1 2.7 %fusion.2 = bf16[256,4096]{1,0:T(8,128)(2,1)} fusion(bf16[1,512,4096]{2,1,0:T(8,128)(2,1)S(1)} %copy-done.4, f32[]{:T(128)} %bitcast.11, f32[1,256,512]{2,1,0:T(8,128)S(1)} %fusion.20), kind=kOutput, calls=%fused_computation.6 | convolution fusion | flops 1077018624 | bytes 6815748 | tf_op jit(solution)/shard_map/bru,bud->brd/dot_general | solution.py:44
  29.8 0.0 reduce-scatter.7.cloned.1.call-start
  29.9 6.3 %all-gather.5.cloned.1.call-done = bf16[1,256,4096]{2,1,0:T(8,128)(2,1)} async-done(((bf16[1,128,4096]{2,1,0:T(8,128)(2,1)}), bf16[1,256,4096]{2,1,0:T(8,128)(2,1)}) %all-gather.5.cloned.1.call-update) | async-done | bytes 2097168 | tf_op jit(solution)/shard_map/all_gather | solution.py:35
  36.2 4.4 %fusion.40 = bf16[256,512]{1,0:T(8,128)(2,1)S(1)} fusion(bf16[1,512,4096]{2,1,0:T(8,128)(2,1)} %param.10, bf16[1,256,4096]{2,1,0:T(8,128)(2,1)} %all-gather.5.cloned.1.call-done, bf16[4096]{0:T(1024)(128)(2,1)S(1)} %fusion.58, f32[1,256,512]{2,1,0:T(8,128)S(1)} %fusion.20), kind=kOutput, calls=%fused_computation.30 | convolution fusion | flops 1077280768 | bytes 7086080 | tf_op jit(solution)/shard_map/rd,bud->bru/dot_general | solution.py:54
  40.6 2.7 %fusion.3 = bf16[256,4096]{1,0:T(8,128)(2,1)} fusion(bf16[256,512]{1,0:T(8,128)(2,1)S(1)} %fusion.40, bf16[1,4096,512]{2,1,0:T(8,128)(2,1)S(1)} %copy-done.5, f32[]{:T(128)} %bitcast.11), kind=kOutput, calls=%fused_computation.7 | convolution fusion | flops 1075838976 | bytes 6553604 | tf_op jit(solution)/shard_map/bru,bdu->brd/dot_general | solution.py:67
  43.4 0.0 reduce-scatter.11.cloned.1.call-start
  43.4 0.6 copy-done.8
  44.0 0.6 dynamic_slice.11
  45.3 3.4 %fusion.1 = bf16[1,512,4096]{2,1,0:T(8,128)(2,1)} fusion(f32[]{:T(128)} %bitcast.21, bf16[1,256,4096]{2,1,0:T(8,128)(2,1)S(1)} %copy-done.6, bf16[4096]{0:T(1024)(128)(2,1)S(1)} %fusion.58, f32[1,256,512]{2,1,0:T(8,128)S(1)} %fusion.20), kind=kOutput, calls=%fused_computation.3 | convolution fusion | flops 1080164352 | bytes 6823940 | tf_op jit(solution)/shard_map/bru,rd->bud/dot_general | solution.py:51
  48.7 0.0 reduce-scatter.9.cloned.1.call-start
  48.8 1.6 copy-done.2
  50.3 3.3 %fusion = bf16[1,4096,512]{1,2,0:T(8,128)(2,1)} fusion(bf16[256,512]{1,0:T(8,128)(2,1)S(1)} %fusion.40, f32[]{:T(128)} %bitcast.21, bf16[1,256,4096]{2,1,0:T(8,128)(2,1)S(1)} %copy-done.2, bf16[4096]{0:T(1024)(128)(2,1)S(1)} %fusion.58), kind=kOutput, calls=%fused_computation.2 | convolution fusion | flops 1078984704 | bytes 6561796 | tf_op jit(solution)/shard_map/rd,bru->bdu/dot_general | solution.py:56
  53.7 8.6 %reduce-scatter.7.cloned.1.call-done = bf16[128,4096]{1,0:T(8,128)(2,1)} async-done(((bf16[256,4096]{1,0:T(8,128)(2,1)}), bf16[128,4096]{1,0:T(8,128)(2,1)}) %reduce-scatter.7.cloned.1.call-update) | async-done | bytes 1048592 | tf_op jit(solution)/shard_map/reduce_scatter | solution.py:68
  62.3 3.6 %fusion.46 = (bf16[1,128,4096]{2,1,0:T(8,128)(2,1)}, bf16[1,128,4096]{2,1,0:T(8,128)(2,1)}) fusion(bf16[128,4096]{1,0:T(8,128)(2,1)} %reduce-scatter.7.cloned.1.call-done, bf16[1,128,4096]{2,1,0:T(8,128)(2,1)S(1)} %copy-done.1, f32[4096]{0:T(1024)S(1)} %fusion.59, bf16[128,4096]{1,0:T(8,128)(2,1)} %reduce-scatter.5.cloned.1.call-done, ...), kind=kLoop, calls=%fused_computation.32 | loop fusion | flops 5242880 | bytes 6307840 | tf_op jit(solution)/shard_map/broadcast_in_dim | solution.py:76
  65.9 94.8 %reduce-scatter.11.cloned.1.call-done = bf16[1,512,256]{2,1,0:T(8,128)(2,1)} async-done(((bf16[1,512,4096]{2,1,0:T(8,128)(2,1)}), bf16[1,512,256]{2,1,0:T(8,128)(2,1)}) %reduce-scatter.11.cloned.1.call-update) | async-done | bytes 262160 | tf_op jit(solution)/shard_map/reduce_scatter | solution.py:63
  160.7 1.8 convert_element_type.106
  162.5 95.1 %reduce-scatter.9.cloned.1.call-done = bf16[1,256,512]{1,2,0:T(8,128)(2,1)} async-done(((bf16[1,4096,512]{1,2,0:T(8,128)(2,1)}), bf16[1,256,512]{1,2,0:T(8,128)(2,1)}) %reduce-scatter.9.cloned.1.call-update) | async-done | bytes 262160 | tf_op jit(solution)/shard_map/reduce_scatter | solution.py:60
  257.6 1.9 copy.11
  (26 shorter events, 0.2 us)
Async XLA Ops:
  7.2 1.6 copy-start.7
  7.2 2.1 copy-start.3
  7.2 15.7 %all-gather.3.cloned.1.call-start = ((), (), s32[]{:S(2)}) async-start(), calls=%async_computation.4 | async-start | bytes 3145728 | tf_op jit(solution)/shard_map/all_gather | solution.py:34
  7.9 28.3 %all-gather.5.cloned.1.call-start = ((), (), s32[]{:S(2)}) async-start(), calls=%async_computation.6 | async-start | bytes 3145728 | tf_op jit(solution)/shard_map/all_gather | solution.py:35
  8.7 45.0 %reduce-scatter.5.cloned.1.call-start = ((), (), s32[]{:S(2)}) async-start(), calls=%async_computation.5 | async-start | bytes 3145728 | tf_op jit(solution)/shard_map/reduce_scatter | solution.py:45
  22.9 4.2 %copy-start.4 = (bf16[1,512,4096]{2,1,0:T(8,128)(2,1)S(1)}, bf16[1,512,4096]{2,1,0:T(8,128)(2,1)}, u32[]{:S(2)}) copy-start(bf16[1,512,4096]{2,1,0:T(8,128)(2,1)} %param.10) | copy-start | bytes 12582916
  29.8 32.4 %reduce-scatter.7.cloned.1.call-start = ((), (), s32[]{:S(2)}) async-start(), calls=%async_computation.7 | async-start | bytes 3145728 | tf_op jit(solution)/shard_map/reduce_scatter | solution.py:68
  36.2 4.4 %copy-start.5 = (bf16[1,4096,512]{2,1,0:T(8,128)(2,1)S(1)}, bf16[1,4096,512]{2,1,0:T(8,128)(2,1)}, u32[]{:S(2)}) copy-start(bf16[1,4096,512]{2,1,0:T(8,128)(2,1)} %param.9) | copy-start | bytes 12582916
  43.4 0.7 copy-start.8
  43.4 1.9 copy-start.6
  43.4 117.3 %reduce-scatter.11.cloned.1.call-start = ((), (), s32[]{:S(2)}) async-start(), calls=%async_computation.9 | async-start | bytes 4456448 | tf_op jit(solution)/shard_map/reduce_scatter | solution.py:63
  48.7 1.6 copy-start.2
  48.7 208.9 %reduce-scatter.9.cloned.1.call-start = ((), (), s32[]{:S(2)}) async-start(), calls=%async_computation.8 | async-start | bytes 4456448 | tf_op jit(solution)/shard_map/reduce_scatter | solution.py:60
  53.6 8.7 %copy-start = (bf16[1,128,4096]{2,1,0:T(8,128)(2,1)S(1)}, bf16[1,128,4096]{2,1,0:T(8,128)(2,1)}, u32[]{:S(2)}) copy-start(bf16[1,128,4096]{2,1,0:T(8,128)(2,1)} %param.7) | copy-start | bytes 3145732
  53.6 8.7 %copy-start.1 = (bf16[1,128,4096]{2,1,0:T(8,128)(2,1)S(1)}, bf16[1,128,4096]{2,1,0:T(8,128)(2,1)}, u32[]{:S(2)}) copy-start(bf16[1,128,4096]{2,1,0:T(8,128)(2,1)} %param.8) | copy-start | bytes 3145732
Sparse Core Ops, SparseCore 0:
  9.6 13.2 all-gather.2
  24.4 11.7 all-gather.4
  38.4 10.7 reduce-scatter.4
  51.4 10.8 reduce-scatter.6
  64.4 96.2 reduce-scatter.10
  162.9 94.6 reduce-scatter.8
where the time goes:
time: 267 us; the launch traced here: 266 us
  waiting for transfers between devices  218 us (82%)
  matrix products  20.7 us (8%)
  between operations  16.2 us (6%)
  local copies, waits for them, and re-layouts  5.8 us (2%)
  other arithmetic  5.43 us (2%)
    reduce_scatter x1, waiting for transfers between devices, local(): lax.psum_scatter(up_term.astype(jnp.bfloat16), 'dp', scatter_dimension=1,...  95.1 us
    reduce_scatter x1, waiting for transfers between devices, local(): lax.psum_scatter(down_term.astype(jnp.bfloat16), 'dp', scatter_dimension=...  94.8 us
    all_gather x1, waiting for transfers between devices, local(): lax.all_gather(tokens, 'block', axis=1, tiled=True)  11.7 us
    reduce_scatter x2, waiting for transfers between devices, local(): lax.psum_scatter(jnp.sum(products * gate_row[:, None, None], axis=0).asty...  8.63 us
    all_gather x1, waiting for transfers between devices, local(): lax.all_gather(cotangent, 'block', axis=1, tiled=True)  6.31 us
  transfers between devices with their start and end apart: 6, of which 5 were waited for; matrix products, arithmetic and copies ran while one was open for 10% of the time, Pallas kernels for 0%

commit v1 on v0

v1 whole, which is shorter than its diff:
```python
import functools
import math

import jax
import jax.numpy as jnp
from jax import lax
from jax.experimental import pallas as pl
from jax.experimental.pallas import tpu as pltpu
from jax.sharding import PartitionSpec as P

GELU_C = math.sqrt(2.0 / math.pi)
GROUP = 4
BF16 = jnp.bfloat16
F32 = jnp.float32


def gelu_parts(v):
    t = jnp.tanh(GELU_C * (v + 0.044715 * v * v * v))
    value = 0.5 * v * (1.0 + t)
    slope = 0.5 * (1.0 + t) + 0.5 * v * (1.0 - t * t) * GELU_C * (1.0 + 3.0 * 0.044715 * v * v)
    return value, slope


def kernel(
    n_dp, n_blk,
    x_hbm, dy_hbm, wu_hbm, wd_hbm, active, width, counts,
    mixed_hbm, ing_hbm, up_hbm, down_hbm,
    x_raw, dy_raw, wu, wd, x_own, y_own, x_all, y_all, h_all, g_all, h_t, g_t, pre, slope,
    out_part, in_part, out_got, in_got, partial, z_send, z_got, mixed_v, ing_v, grad_v,
    loc, sib_s, sib_r, a2a_s, a2a_r, fwd_s, fwd_r, gat_s, gat_r, rel_s, rel_r, red_s, red_r, zs, zr,
):
    me = lax.axis_index("dp")
    blk = lax.axis_index("block")
    steps = n_dp // GROUP
    rows_own, feats = x_raw.shape
    units = wu.shape[1]
    rows = rows_own * n_blk
    half = rows // 2
    chunk = feats // n_dp
    hi = lax.div(me, GROUP)
    lo = lax.rem(me, GROUP)
    lx = lax.rem(lo, 2)
    ly = lax.div(lo, 2)

    def mate(o):
        px = 1 - lx if o & 1 else lx
        py = 1 - ly if o & 2 else ly
        return py * 2 + px

    def at(dp, b):
        return {"dp": dp, "block": b}

    mesh_id = pl.DeviceIdType.MESH
    mates = {o: mate(o) for o in range(1, GROUP)}
    mate_id = {o: at(hi * GROUP + mates[o], blk) for o in mates}
    sibs = {k: lax.rem(blk + k, n_blk) for k in range(1, n_blk)}
    sib_id = {k: at(me, sibs[k]) for k in sibs}
    side_id = (at(me + GROUP, blk), at(me - GROUP, blk))
    has_right = hi < steps - 1
    has_left = hi > 0
    mine = pl.ds(pl.multiple_of(blk * rows_own, rows_own), rows_own)

    loads = [
        pltpu.make_async_copy(s, d, loc.at[i])
        for i, (s, d) in enumerate(((x_hbm, x_raw), (dy_hbm, dy_raw), (wu_hbm, wu), (wd_hbm, wd)))
    ]
    for c in loads:
        c.start()

    barrier = pltpu.get_barrier_semaphore()
    for dev in list(mate_id.values()) + list(sib_id.values()):
        pl.semaphore_signal(barrier, inc=1, device_id=dev, device_id_type=mesh_id)

    @pl.when(has_right)
    def _():
        pl.semaphore_signal(barrier, inc=1, device_id=side_id[0], device_id_type=mesh_id)

    @pl.when(has_left)
    def _():
        pl.semaphore_signal(barrier, inc=1, device_id=side_id[1], device_id_type=mesh_id)

    pl.semaphore_wait(
        barrier,
        len(mate_id) + len(sib_id) + has_right.astype(jnp.int32) + has_left.astype(jnp.int32),
    )

    def remote(src, dst, s, r, dev):
        return pltpu.make_async_remote_copy(
            src_ref=src, dst_ref=dst, send_sem=s, recv_sem=r, device_id=dev, device_id_type=mesh_id
        )

    limit = feats // 16 * width[me]
    gate = active[me, blk].astype(F32)
    inv = 1.0 / counts[blk].astype(F32)

    def chunk_mask(start, size, kind):
        col = lax.broadcasted_iota(jnp.int32, (1, size), 1) + start
        return jnp.where(col < limit, 1.0, 0.0).astype(kind)

    def mask_into(raw, own):
        for l in range(GROUP):
            for h in range(steps):
                c = h * GROUP + l
                own[l, h, mine, :] = raw[:, c * chunk:(c + 1) * chunk] * chunk_mask(c * chunk, chunk, BF16)

    def share(t, own):
        out = []
        for k in sibs:
            cp = remote(own.at[:, :, mine, :], own.at[:, :, mine, :], sib_s.at[t, k], sib_r.at[t, k], sib_id[k])
            cp.start()
            out.append(cp)
        return out

    def spread(t, own, every):
        out = {}
        for o in mates:
            cp = remote(
                own.at[mates[o], :, mine, :], every.at[:, o, mine, :], a2a_s.at[t, o], a2a_r.at[t, o], mate_id[o]
            )
            cp.start()
            out[o] = cp
        return out

    def forward(t, every, copies):
        out = []
        for o in (1, 2, 3):
            copies[o].wait_recv()
            for k in sibs:
                cp = remote(
                    every.at[:, o, mine, :], every.at[:, o, mine, :], fwd_s.at[t, o, k], fwd_r.at[t, o, k], sib_id[k]
                )
                cp.start()
                out.append(cp)
        return out

    def gather(t, every):
        out = {}
        for o in (1, 2):
            cp = remote(every.at[0], every.at[o], gat_s.at[t, o], gat_r.at[t, o], mate_id[o])
            cp.start()
            out[o] = cp
        return out

    def relay(t, every, copies):
        out = []
        for o, lo_row in ((1, 0), (2, half)):
            copies[o].wait_recv()
            part = pl.ds(lo_row, half)
            cp = remote(every.at[o, part], every.at[3, part], rel_s.at[t, o], rel_r.at[t, o], mate_id[3 - o])
            cp.start()
            out.append(cp)
        return out

    def to_owner(t, parts, got):
        out = []
        for k in sibs:
            theirs = pl.ds(pl.multiple_of(sibs[k] * rows_own, rows_own), rows_own)
            cp = remote(parts.at[theirs], got.at[k - 1], red_s.at[t, k], red_r.at[t, k], sib_id[k])
            cp.start()
            out.append(cp)
        return out

    loads[0].wait()
    mask_into(x_raw, x_own)
    sib_x = share(0, x_own)
    loads[1].wait()
    mask_into(dy_raw, y_own)
    a2a_y = spread(1, y_own, y_all)
    sib_y = share(1, y_own)

    loads[2].wait()
    for cp in sib_x:
        cp.wait_recv()
    acc = None
    for l in range(GROUP):
        for h in range(steps):
            c = h * GROUP + l
            term = jnp.dot(x_own[l, h], wu[c * chunk:(c + 1) * chunk, :], preferred_element_type=F32)
            acc = term if acc is None else acc + term
    pre[...] = acc

    piece = 32

    def gelu_step(i, carry):
        r = pl.ds(pl.multiple_of(i * piece, piece), piece)
        value, sl = gelu_parts(pre[r, :])
        h_all[0, r, :] = (value * gate).astype(BF16)
        slope[r, :] = sl
        return carry

    lax.fori_loop(0, rows // piece, gelu_step, 0)
    gat_h = gather(0, h_all)
    a2a_x = spread(0, x_own, x_all)

    loads[3].wait()
    for cp in sib_y:
        cp.wait_recv()
    acc = None
    nt = (((1,), (1,)), ((), ()))
    for l in range(GROUP):
        for h in range(steps):
            c = h * GROUP + l
            term = lax.dot_general(
                y_own[l, h], wd[:, c * chunk:(c + 1) * chunk], nt, preferred_element_type=F32
            )
            acc = term if acc is None else acc + term
    g_all[0] = (acc * slope[...]).astype(BF16) * gate.astype(BF16)
    gat_g = gather(1, g_all)

    wide = 512

    def out_step(j, carry):
        cols = pl.ds(pl.multiple_of(j * wide, wide), wide)
        out_part[:, cols] = jnp.dot(h_all[0], wd[:, cols], preferred_element_type=F32).astype(BF16)
        return carry

    lax.fori_loop(0, feats // wide, out_step, 0)
    own_out = to_owner(0, out_part, out_got)
    h_t[:, 0:rows] = h_all[0].T
    for h in range(steps):
        y_all[h, 0] = y_own[lo, h]

    rel_h = relay(0, h_all, gat_h)
    fwd_y = forward(1, y_all, a2a_y)

    def in_step(j, carry):
        cols = pl.ds(pl.multiple_of(j * wide, wide), wide)
        in_part[:, cols] = lax.dot_general(
            g_all[0], wu[cols, :], nt, preferred_element_type=F32
        ).astype(BF16)
        return carry

    lax.fori_loop(0, feats // wide, in_step, 0)
    own_in = to_owner(1, in_part, in_got)
    g_t[:, 0:rows] = g_all[0].T
    for h in range(steps):
        x_all[h, 0] = x_own[lo, h]
    for o in (1, 2):
        h_t[:, o * rows:(o + 1) * rows] = h_all[o].T

    def finish(parts, got, raw, held, copies):
        for cp in copies:
            cp.wait_recv()

        def step(j, carry):
            cols = pl.ds(pl.multiple_of(j * wide, wide), wide)
            total = parts[mine, cols].astype(F32)
            for k in sibs:
                total = total + got[k - 1, :, cols].astype(F32)
            held[:, cols] = (raw[:, cols].astype(F32) + chunk_mask(j * wide, wide, F32) * total).astype(BF16)
            return carry

        lax.fori_loop(0, feats // wide, step, 0)

    finish(out_part, out_got, x_raw, mixed_v, own_out)
    store_mixed = pltpu.make_async_copy(mixed_v, mixed_hbm, loc.at[4])
    store_mixed.start()

    def partials(t, every_t, every):
        def step(h, carry):
            block = every[h].reshape(GROUP * rows, chunk)
            partial[t, h] = jnp.dot(every_t[...], block, preferred_element_type=F32)
            return carry

        lax.fori_loop(0, steps, step, 0)

    def z_copy(t, side, d):
        return remote(
            z_send.at[t, side, d - 1], z_got.at[t, side, d - 1], zs.at[t, side, d - 1], zr.at[t, side, d - 1],
            side_id[side],
        )

    def z_conditions(side, d):
        sends = hi + d <= steps - 1 if side == 0 else hi - d >= 0
        behind = has_left if side == 0 else has_right
        return sends, behind

    def chain(t):
        for d in range(steps - 1, 0, -1):
            for side in (0, 1):
                sends, behind = z_conditions(side, d)

                @pl.when(sends)
                def _():
                    target = hi + d if side == 0 else hi - d
                    if d == steps - 1:
                        z_send[t, side, d - 1] = partial[t, target].astype(BF16)
                    else:
                        @pl.when(behind)
                        def _():
                            z_copy(t, side, d + 1).wait_recv()
                            z_send[t, side, d - 1] = (
                                partial[t, target] + z_got[t, side, d].astype(F32)
                            ).astype(BF16)

                        @pl.when(jnp.logical_not(behind))
                        def _():
                            z_send[t, side, d - 1] = partial[t, target].astype(BF16)

                    z_copy(t, side, d).start()

    def close(t):
        for side, behind in ((0, has_left), (1, has_right)):
            @pl.when(behind)
            def _():
                z_copy(t, side, 1).wait_recv()
                partial[t, hi] = partial[t, hi] + z_got[t, side, 0].astype(F32)

        return partial[t, hi] * inv

    for cp in rel_h:
        cp.wait_recv()
    h_t[:, 3 * rows:] = h_all[3].T
    for cp in fwd_y:
        cp.wait_recv()
    partials(0, h_t, y_all)
    chain(0)

    rel_g = relay(1, g_all, gat_g)
    fwd_x = forward(0, x_all, a2a_x)
    for o in (1, 2):
        g_t[:, o * rows:(o + 1) * rows] = g_all[o].T
    finish(in_part, in_got, dy_raw, ing_v, own_in)
    store_ing = pltpu.make_async_copy(ing_v, ing_hbm, loc.at[5])
    store_ing.start()

    for cp in rel_g:
        cp.wait_recv()
    g_t[:, 3 * rows:] = g_all[3].T
    for cp in fwd_x:
        cp.wait_recv()
    partials(1, g_t, x_all)
    chain(1)

    grad_v[...] = close(0)
    store_down = pltpu.make_async_copy(grad_v, down_hbm, loc.at[6])
    store_down.start()
    pre_t = close(1)
    up_v = pre.at[0:chunk, :]
    up_v[...] = pre_t.T
    store_up = pltpu.make_async_copy(up_v, up_hbm, loc.at[7])
    store_up.start()

    for cp in sib_x + sib_y + own_out + own_in + fwd_x + fwd_y + rel_h + rel_g:
        cp.wait_send()
    for group in (a2a_x, a2a_y, gat_h, gat_g):
        for cp in group.values():
            cp.wait_send()
    for t in (0, 1):
        for d in range(steps - 1, 0, -1):
            for side in (0, 1):
                sends, _ = z_conditions(side, d)

                @pl.when(sends)
                def _():
                    z_copy(t, side, d).wait_send()
    for cp in (store_mixed, store_ing, store_down, store_up):
        cp.wait()


def local(n_dp, n_blk, tokens, cotangent, w_up, w_down, active, width, counts):
    _, rows_own, feats = tokens.shape
    units = w_up.shape[2]
    rows = rows_own * n_blk
    chunk = feats // n_dp
    steps = n_dp // GROUP
    hops = max(steps - 1, 1)
    dma = pltpu.SemaphoreType.DMA
    anywhere = pl.BlockSpec(memory_space=pl.ANY)
    scalars = pl.BlockSpec(memory_space=pltpu.SMEM)
    scratch = [
        pltpu.VMEM((rows_own, feats), BF16),
        pltpu.VMEM((rows_own, feats), BF16),
        pltpu.VMEM((feats, units), BF16),
        pltpu.VMEM((units, feats), BF16),
        pltpu.VMEM((GROUP, steps, rows, chunk), BF16),
        pltpu.VMEM((GROUP, steps, rows, chunk), BF16),
        pltpu.VMEM((steps, GROUP, rows, chunk), BF16),
        pltpu.VMEM((steps, GROUP, rows, chunk), BF16),
        pltpu.VMEM((GROUP, rows, units), BF16),
        pltpu.VMEM((GROUP, rows, units), BF16),
        pltpu.VMEM((units, GROUP * rows), BF16),
        pltpu.VMEM((units, GROUP * rows), BF16),
        pltpu.VMEM((rows, units), F32),
        pltpu.VMEM((rows, units), F32),
        pltpu.VMEM((rows, feats), BF16),
        pltpu.VMEM((rows, feats), BF16),
        pltpu.VMEM((n_blk - 1, rows_own, feats), BF16),
        pltpu.VMEM((n_blk - 1, rows_own, feats), BF16),
        pltpu.VMEM((2, steps, units, chunk), F32),
        pltpu.VMEM((2, 2, hops, units, chunk), BF16),
        pltpu.VMEM((2, 2, hops, units, chunk), BF16),
        pltpu.VMEM((rows_own, feats), BF16),
        pltpu.VMEM((rows_own, feats), BF16),
        pltpu.VMEM((units, chunk), F32),
        dma((8,)),
        dma((2, n_blk)), dma((2, n_blk)),
        dma((2, GROUP)), dma((2, GROUP)),
        dma((2, GROUP, n_blk)), dma((2, GROUP, n_blk)),
        dma((2, GROUP)), dma((2, GROUP)),
        dma((2, GROUP)), dma((2, GROUP)),
        dma((2, n_blk)), dma((2, n_blk)),
        dma((2, 2, hops)), dma((2, 2, hops)),
    ]
    mixed, ing, up, down = pl.pallas_call(
        functools.partial(kernel, n_dp, n_blk),
        out_shape=(
            jax.ShapeDtypeStruct((rows_own, feats), BF16),
            jax.ShapeDtypeStruct((rows_own, feats), BF16),
            jax.ShapeDtypeStruct((chunk, units), F32),
            jax.ShapeDtypeStruct((units, chunk), F32),
        ),
        in_specs=[anywhere] * 4 + [scalars] * 3,
        out_specs=(anywhere,) * 4,
        scratch_shapes=scratch,
        compiler_params=pltpu.CompilerParams(
            collective_id=0, has_side_effects=True, vmem_limit_bytes=60 * 1024 * 1024
        ),
        cost_estimate=pl.CostEstimate(
            flops=12 * rows * feats * units, bytes_accessed=16 * 1024 * 1024, transcendentals=rows * units
        ),
    )(tokens[0], cotangent[0], w_up[0], w_down[0], active, width, counts)
    return mixed[None], ing[None], up[None], down[None]


def solution(mesh):
    in_specs = (
        P("dp", "block", None),
        P("dp", "block", None),
        P("block", None, None),
        P("block", None, None),
        P(),
        P(),
        P(),
    )
    out_specs = (
        P("dp", "block", None),
        P("dp", "block", None),
        P("block", "dp", None),
        P("block", None, "dp"),
    )
    body = functools.partial(local, mesh.shape["dp"], mesh.shape["block"])
    return jax.shard_map(body, mesh=mesh, in_specs=in_specs, out_specs=out_specs, check_vma=False)
```

time: 267 us -> 93.9 us (0.35)
  waiting for transfers between devices: 218 us -> 0 us
  Pallas kernels: 0 us -> 85.4 us
  matrix products: 20.7 us -> 0 us
  between operations: 16.2 us -> 0.66 us
  other arithmetic: 5.43 us -> 0 us
    reduce_scatter x4 -> x0, waiting for transfers between devices: 199 us -> none  [the longest x1 95.1 us: local(): lax.psum_scatter(up_term.astype(jnp.bfloat16), 'dp', scatter_dimension=1,...]
    pallas_call x0 -> x1, Pallas kernels: none -> 85.4 us  [local(): pl.pallas_call(functools.partial(kernel, n_dp, n_blk), out_shape=(jax.Sha...]
    dot_general x6 -> x0, matrix products: 20.7 us -> none  [the longest x1 4.43 us: local(): jnp.einsum('rd,bud->bru', masked_dy, w_down, preferred_element_type=jnp.f...]
    all_gather x2 -> x0, waiting for transfers between devices: 18 us -> none  [the longest x1 11.7 us: local(): lax.all_gather(tokens, 'block', axis=1, tiled=True)]
    broadcast_in_dim x1 -> x0, other arithmetic: 3.64 us -> none  [local(): (cotangent[0].astype(jnp.float32) + mask_float * input_sum).astype(jnp.bf...]
    unnamed x19 -> x9, local copies, waits for them, and re-layouts: 4.05 us -> 7.61 us
  transfers between devices with their start and end apart: 6 -> 0, of which waited for: 5 -> 0; matrix products, arithmetic and copies ran while one was open for 10% -> 0% of each run, Pallas kernels for 0% -> 0%
where the time goes in v1:
time: 93.9 us; the launch traced here: 93.6 us
  Pallas kernels  85.4 us (91%)
  local copies, waits for them, and re-layouts  7.61 us (8%)
    pallas_call x1, Pallas kernels, local(): pl.pallas_call(functools.partial(kernel, n_dp, n_blk), out_shape=(jax.Sha...  85.4 us
    unnamed x9, local copies, waits for them, and re-layouts  7.61 us

profile of v1, /device:TPU:0, one launch (start us, length us, event | category | flops | bytes accessed | tf_op | source)
XLA Modules:
  0.0 93.6 jit_solution(9895540948531206801)
XLA Ops:
  0.6 1.4 %copy.11.active = s32[16,2]{1,0:T(8,128)} copy(s32[16,2]{0,1:T(2,128)} %param.11) | data formatting | bytes 256 | tf_op args[4]
  2.0 85.4 %shard_map.102 = (bf16[128,4096]{1,0:T(8,128)(2,1)}, bf16[128,4096]{1,0:T(8,128)(2,1)}, f32[256,512]{1,0:T(8,128)}, f32[512,256]{1,0:T(8,128)}) custom-call(bf16[128,4096]{1,0:T(8,128)(2,1)} %bitcast.14, bf16[128,4096]{1,0:T(8,128)(2,1)} %bitcast.15, bf16[4096,512]{1,0:T(8,128)(2,1)} %bitcast.12, bf16[512,4096]{1,0:T(8,128)(2,1)} %bitcast.13, ...), custom_call_target="tpu_custom_call" | custom-call | flops 6442450944 | bytes 16777216 | tf_op jit(solution)/shard_map/pallas_call | solution.py:405
  87.4 0.0 copy-start.1
  87.4 0.0 copy-start
  87.4 2.4 %copy.16 = bf16[1,128,4096]{2,1,0:T(8,128)(2,1)} copy(bf16[1,128,4096]{2,1,0:T(8,128)(2,1)} %bitcast.9) | data formatting | bytes 2097152
  89.8 2.3 %copy.17 = bf16[1,128,4096]{2,1,0:T(8,128)(2,1)} copy(bf16[1,128,4096]{2,1,0:T(8,128)(2,1)} %bitcast.8) | data formatting | bytes 2097152
  92.0 0.0 copy-done.1
  92.1 0.8 copy.18
  92.8 0.0 copy-done
  92.8 0.8 copy.19
Async XLA Ops:
  87.4 4.7 %copy-start.1 = (f32[256,512]{1,0:T(8,128)S(1)}, f32[256,512]{1,0:T(8,128)}, u32[]{:S(2)}) copy-start(f32[256,512]{1,0:T(8,128)} %get-tuple-element.10) | copy-start | bytes 1572868
  87.4 5.5 %copy-start = (f32[512,256]{1,0:T(8,128)S(1)}, f32[512,256]{1,0:T(8,128)}, u32[]{:S(2)}) copy-start(f32[512,256]{1,0:T(8,128)} %get-tuple-element.11) | copy-start | bytes 1572868

commit v2 on v1

--- a/solution.py
+++ b/solution.py
@@ -64,8 +64,8 @@
         pltpu.make_async_copy(s, d, loc.at[i])
         for i, (s, d) in enumerate(((x_hbm, x_raw), (dy_hbm, dy_raw), (wu_hbm, wu), (wd_hbm, wd)))
     ]
-    for c in loads:
-        c.start()
+    loads[1].start()
+    loads[0].start()
 
     barrier = pltpu.get_barrier_semaphore()
     for dev in list(mate_id.values()) + list(sib_id.values()):
@@ -78,11 +78,6 @@
     @pl.when(has_left)
     def _():
         pl.semaphore_signal(barrier, inc=1, device_id=side_id[1], device_id_type=mesh_id)
-
-    pl.semaphore_wait(
-        barrier,
-        len(mate_id) + len(sib_id) + has_right.astype(jnp.int32) + has_left.astype(jnp.int32),
-    )
 
     def remote(src, dst, s, r, dev):
         return pltpu.make_async_remote_copy(
@@ -90,7 +85,7 @@
         )
 
     limit = feats // 16 * width[me]
-    gate = active[me, blk].astype(F32)
+    gate = active[blk, me].astype(F32)
     inv = 1.0 / counts[blk].astype(F32)
 
     def chunk_mask(start, size, kind):
@@ -111,27 +106,46 @@
             out.append(cp)
         return out
 
+    def z_conditions(side, d):
+        sends = hi + d <= steps - 1 if side == 0 else hi - d >= 0
+        behind = has_left if side == 0 else has_right
+        return sends, behind
+
+    def in_order(visit):
+        for d in range(steps - 1, 0, -1):
+            for side in (0, 1):
+                @pl.when(z_conditions(side, d)[0])
+                def _():
+                    visit(hi + d if side == 0 else hi - d)
+
+        visit(hi)
+
+    def a2a_copy(t, own, every, o, h):
+        return remote(
+            own.at[mates[o], h, mine, :], every.at[h, o, mine, :], a2a_s.at[t, o, h], a2a_r.at[t, o, h], mate_id[o]
+        )
+
     def spread(t, own, every):
-        out = {}
+        def visit(h):
+            for o in mates:
+                a2a_copy(t, own, every, o, h).start()
+
+        in_order(visit)
+
+    def fwd_copy(t, every, o, h, k):
+        part = every.at[h, o, mine, :]
+        return remote(part, part, fwd_s.at[t, o, h, k], fwd_r.at[t, o, h, k], sib_id[k])
+
+    def forward(t, own, every, h):
         for o in mates:
-            cp = remote(
-                own.at[mates[o], :, mine, :], every.at[:, o, mine, :], a2a_s.at[t, o], a2a_r.at[t, o], mate_id[o]
-            )
-            cp.start()
-            out[o] = cp
-        return out
-
-    def forward(t, every, copies):
-        out = []
-        for o in (1, 2, 3):
-            copies[o].wait_recv()
+            a2a_copy(t, own, every, o, h).wait_recv()
             for k in sibs:
-                cp = remote(
-                    every.at[:, o, mine, :], every.at[:, o, mine, :], fwd_s.at[t, o, k], fwd_r.at[t, o, k], sib_id[k]
-                )
-                cp.start()
-                out.append(cp)
-        return out
+                fwd_copy(t, every, o, h, k).start()
+
+    def forwarded(t, every, h):
+        for o in mates:
+            for k in sibs:
+                fwd_copy(t, every, o, h, k).wait_recv()
 
     def gather(t, every):
         out = {}
@@ -160,12 +174,19 @@
             out.append(cp)
         return out
 
+    loads[1].wait()
+    loads[2].start()
+    loads[3].start()
+    mask_into(dy_raw, y_own)
+    pl.semaphore_wait(
+        barrier,
+        len(mate_id) + len(sib_id) + has_right.astype(jnp.int32) + has_left.astype(jnp.int32),
+    )
+
+    spread(1, y_own, y_all)
     loads[0].wait()
     mask_into(x_raw, x_own)
     sib_x = share(0, x_own)
-    loads[1].wait()
-    mask_into(dy_raw, y_own)
-    a2a_y = spread(1, y_own, y_all)
     sib_y = share(1, y_own)
 
     loads[2].wait()
@@ -190,7 +211,6 @@
 
     lax.fori_loop(0, rows // piece, gelu_step, 0)
     gat_h = gather(0, h_all)
-    a2a_x = spread(0, x_own, x_all)
 
     loads[3].wait()
     for cp in sib_y:
@@ -205,7 +225,6 @@
             )
             acc = term if acc is None else acc + term
     g_all[0] = (acc * slope[...]).astype(BF16) * gate.astype(BF16)
-    gat_g = gather(1, g_all)
 
     wide = 512
 
@@ -221,7 +240,7 @@
         y_all[h, 0] = y_own[lo, h]
 
     rel_h = relay(0, h_all, gat_h)
-    fwd_y = forward(1, y_all, a2a_y)
+    gat_g = gather(1, g_all)
 
     def in_step(j, carry):
         cols = pl.ds(pl.multiple_of(j * wide, wide), wide)
@@ -256,13 +275,14 @@
     store_mixed = pltpu.make_async_copy(mixed_v, mixed_hbm, loc.at[4])
     store_mixed.start()
 
-    def partials(t, every_t, every):
-        def step(h, carry):
-            block = every[h].reshape(GROUP * rows, chunk)
-            partial[t, h] = jnp.dot(every_t[...], block, preferred_element_type=F32)
-            return carry
-
-        lax.fori_loop(0, steps, step, 0)
+    def partial_of(t, h):
+        if t == 0:
+            each_t, own, every = h_t, y_own, y_all
+        else:
+            each_t, own, every = g_t, x_own, x_all
+        forward(1 - t, own, every, h)
+        forwarded(1 - t, every, h)
+        return jnp.dot(each_t[...], every[h].reshape(GROUP * rows, chunk), preferred_element_type=F32)
 
     def z_copy(t, side, d):
         return remote(
@@ -270,54 +290,46 @@
             side_id[side],
         )
 
-    def z_conditions(side, d):
-        sends = hi + d <= steps - 1 if side == 0 else hi - d >= 0
-        behind = has_left if side == 0 else has_right
-        return sends, behind
-
-    def chain(t):
+    def chain(t, between):
         for d in range(steps - 1, 0, -1):
+            if d == 1:
+                between()
             for side in (0, 1):
                 sends, behind = z_conditions(side, d)
 
                 @pl.when(sends)
                 def _():
-                    target = hi + d if side == 0 else hi - d
-                    if d == steps - 1:
-                        z_send[t, side, d - 1] = partial[t, target].astype(BF16)
-                    else:
+                    partial[t] = partial_of(t, hi + d if side == 0 else hi - d)
+                    if d < steps - 1:
                         @pl.when(behind)
                         def _():
                             z_copy(t, side, d + 1).wait_recv()
-                            z_send[t, side, d - 1] = (
-                                partial[t, target] + z_got[t, side, d].astype(F32)
-                            ).astype(BF16)
-
-                        @pl.when(jnp.logical_not(behind))
-                        def _():
-                            z_send[t, side, d - 1] = partial[t, target].astype(BF16)
-
+                            partial[t] = partial[t] + z_got[t, side, d].astype(F32)
+
+                    z_send[t, side, d - 1] = partial[t].astype(BF16)
                     z_copy(t, side, d).start()
+
+        partial[t] = partial_of(t, hi)
 
     def close(t):
         for side, behind in ((0, has_left), (1, has_right)):
             @pl.when(behind)
             def _():
                 z_copy(t, side, 1).wait_recv()
-                partial[t, hi] = partial[t, hi] + z_got[t, side, 0].astype(F32)
-
-        return partial[t, hi] * inv
-
+                partial[t] = partial[t] + z_got[t, side, 0].astype(F32)
+
+        return partial[t] * inv
+
+    def pass_on():
+        rel_g.extend(relay(1, g_all, gat_g))
+        spread(0, x_own, x_all)
+
+    rel_g = []
     for cp in rel_h:
         cp.wait_recv()
     h_t[:, 3 * rows:] = h_all[3].T
-    for cp in fwd_y:
-        cp.wait_recv()
-    partials(0, h_t, y_all)
-    chain(0)
-
-    rel_g = relay(1, g_all, gat_g)
-    fwd_x = forward(0, x_all, a2a_x)
+    chain(0, pass_on)
+
     for o in (1, 2):
         g_t[:, o * rows:(o + 1) * rows] = g_all[o].T
     finish(in_part, in_got, dy_raw, ing_v, own_in)
@@ -327,10 +339,7 @@
     for cp in rel_g:
         cp.wait_recv()
     g_t[:, 3 * rows:] = g_all[3].T
-    for cp in fwd_x:
-        cp.wait_recv()
-    partials(1, g_t, x_all)
-    chain(1)
+    chain(1, lambda: None)
 
     grad_v[...] = close(0)
     store_down = pltpu.make_async_copy(grad_v, down_hbm, loc.at[6])
@@ -341,9 +350,19 @@
     store_up = pltpu.make_async_copy(up_v, up_hbm, loc.at[7])
     store_up.start()
 
-    for cp in sib_x + sib_y + own_out + own_in + fwd_x + fwd_y + rel_h + rel_g:
+    for cp in sib_x + sib_y + own_out + own_in + rel_h + rel_g:
         cp.wait_send()
-    for group in (a2a_x, a2a_y, gat_h, gat_g):
+
+    def drain(h, carry):
+        for t, own, every in ((0, x_own, x_all), (1, y_own, y_all)):
+            for o in mates:
+                a2a_copy(t, own, every, o, h).wait_send()
+                for k in sibs:
+                    fwd_copy(t, every, o, h, k).wait_send()
+        return carry
+
+    lax.fori_loop(0, steps, drain, 0)
+    for group in (gat_h, gat_g):
         for cp in group.values():
             cp.wait_send()
     for t in (0, 1):
@@ -355,6 +374,20 @@
                 def _():
                     z_copy(t, side, d).wait_send()
     for cp in (store_mixed, store_ing, store_down, store_up):
+        cp.wait()
+
+
+def hand_over(*refs):
+    copies = []
+    sems = refs[-1]
+    for i in range(4):
+        size = refs[i].shape[1] // 2
+        for j in range(2):
+            part = pl.ds(j * size, size)
+            copies.append(pltpu.make_async_copy(refs[i].at[:, part], refs[4 + i].at[:, part], sems.at[i, j]))
+    for cp in copies:
+        cp.start()
+    for cp in copies:
         cp.wait()
 
 
@@ -387,7 +420,7 @@
         pltpu.VMEM((rows, feats), BF16),
         pltpu.VMEM((n_blk - 1, rows_own, feats), BF16),
         pltpu.VMEM((n_blk - 1, rows_own, feats), BF16),
-        pltpu.VMEM((2, steps, units, chunk), F32),
+        pltpu.VMEM((2, units, chunk), F32),
         pltpu.VMEM((2, 2, hops, units, chunk), BF16),
         pltpu.VMEM((2, 2, hops, units, chunk), BF16),
         pltpu.VMEM((rows_own, feats), BF16),
@@ -395,8 +428,8 @@
         pltpu.VMEM((units, chunk), F32),
         dma((8,)),
         dma((2, n_blk)), dma((2, n_blk)),
-        dma((2, GROUP)), dma((2, GROUP)),
-        dma((2, GROUP, n_blk)), dma((2, GROUP, n_blk)),
+        dma((2, GROUP, steps)), dma((2, GROUP, steps)),
+        dma((2, GROUP, steps, n_blk)), dma((2, GROUP, steps, n_blk)),
         dma((2, GROUP)), dma((2, GROUP)),
         dma((2, GROUP)), dma((2, GROUP)),
         dma((2, n_blk)), dma((2, n_blk)),
@@ -419,8 +452,15 @@
         cost_estimate=pl.CostEstimate(
             flops=12 * rows * feats * units, bytes_accessed=16 * 1024 * 1024, transcendentals=rows * units
         ),
-    )(tokens[0], cotangent[0], w_up[0], w_down[0], active, width, counts)
-    return mixed[None], ing[None], up[None], down[None]
+    )(tokens[0], cotangent[0], w_up[0], w_down[0], active.T, width, counts)
+    results = (mixed[None], ing[None], up[None], down[None])
+    return pl.pallas_call(
+        hand_over,
+        out_shape=tuple(jax.ShapeDtypeStruct(r.shape, r.dtype) for r in results),
+        in_specs=[anywhere] * 4,
+        out_specs=(anywhere,) * 4,
+        scratch_shapes=[dma((4, 2))],
+    )(*results)
 
 
 def solution(mesh):

time: 93.9 us -> 171 us (1.82)
  Pallas kernels: 85.4 us -> 170 us
  local copies, waits for them, and re-layouts: 7.61 us -> 0 us
    pallas_call x0 -> x1, Pallas kernels: none -> 96.5 us  [local(): pl.pallas_call(hand_over, out_shape=tuple((jax.ShapeDtypeStruct(r.shape,...]
    pallas_call x1, Pallas kernels: 85.4 us -> 74 us  [local(): pl.pallas_call(functools.partial(kernel, n_dp, n_blk), out_shape=(jax.Sha...]
    unnamed x9 -> x0, local copies, waits for them, and re-layouts: 7.61 us -> none
where the time goes in v2:
time: 171 us
  Pallas kernels  170 us (99%)
    pallas_call x1, Pallas kernels, local(): pl.pallas_call(hand_over, out_shape=tuple((jax.ShapeDtypeStruct(r.shape,...  96.5 us
    pallas_call x1, Pallas kernels, local(): pl.pallas_call(functools.partial(kernel, n_dp, n_blk), out_shape=(jax.Sha...  74 us

profile of v2, /device:TPU:0, one launch (start us, length us, event | category | flops | bytes accessed | tf_op | source)
XLA Modules:
  0.0 171.1 jit_solution(9764295401135531597)
XLA Ops:
  0.6 74.0 %shard_map.102 = (bf16[128,4096]{1,0:T(8,128)(2,1)}, bf16[128,4096]{1,0:T(8,128)(2,1)}, f32[256,512]{1,0:T(8,128)}, f32[512,256]{1,0:T(8,128)}) custom-call(bf16[128,4096]{1,0:T(8,128)(2,1)} %bitcast.15, bf16[128,4096]{1,0:T(8,128)(2,1)} %bitcast.16, bf16[4096,512]{1,0:T(8,128)(2,1)} %bitcast.13, bf16[512,4096]{1,0:T(8,128)(2,1)} %bitcast.14, ...), custom_call_target="tpu_custom_call" | custom-call | flops 6442450944 | bytes 16777216 | tf_op jit(solution)/shard_map/pallas_call | solution.py:438
  74.6 96.5 %shard_map.103 = (bf16[1,128,4096]{2,1,0:T(8,128)(2,1)}, bf16[1,128,4096]{2,1,0:T(8,128)(2,1)}, f32[1,256,512]{2,1,0:T(8,128)}, f32[1,512,256]{2,1,0:T(8,128)}) custom-call(bf16[1,128,4096]{2,1,0:T(8,128)(2,1)} %bitcast.9, bf16[1,128,4096]{2,1,0:T(8,128)(2,1)} %bitcast.10, f32[1,256,512]{2,1,0:T(8,128)} %bitcast.11, f32[1,512,256]{2,1,0:T(8,128)} %bitcast.12), custom_call_target="tpu_custom_call" | custom-call | tf_op jit(solution)/shard_map/pallas_call | solution.py:457

commit v3 on v2

--- a/solution.py
+++ b/solution.py
@@ -36,6 +36,7 @@
     units = wu.shape[1]
     rows = rows_own * n_blk
     half = rows // 2
+    wing = units // 2
     chunk = feats // n_dp
     hi = lax.div(me, GROUP)
     lo = lax.rem(me, GROUP)
@@ -64,8 +65,8 @@
         pltpu.make_async_copy(s, d, loc.at[i])
         for i, (s, d) in enumerate(((x_hbm, x_raw), (dy_hbm, dy_raw), (wu_hbm, wu), (wd_hbm, wd)))
     ]
+    loads[0].start()
     loads[1].start()
-    loads[0].start()
 
     barrier = pltpu.get_barrier_semaphore()
     for dev in list(mate_id.values()) + list(sib_id.values()):
@@ -111,26 +112,21 @@
         behind = has_left if side == 0 else has_right
         return sends, behind
 
-    def in_order(visit):
-        for d in range(steps - 1, 0, -1):
-            for side in (0, 1):
-                @pl.when(z_conditions(side, d)[0])
-                def _():
-                    visit(hi + d if side == 0 else hi - d)
-
-        visit(hi)
+    near = steps // 2
+    low = (hi < near).astype(jnp.int32)
+    base = (1 - low) * near
+    order = [low * (steps - 1 - i) + (1 - low) * i for i in range(near)]
+    order += [base + lax.rem(hi - base + 1 + i, near) for i in range(near)]
 
     def a2a_copy(t, own, every, o, h):
         return remote(
             own.at[mates[o], h, mine, :], every.at[h, o, mine, :], a2a_s.at[t, o, h], a2a_r.at[t, o, h], mate_id[o]
         )
 
-    def spread(t, own, every):
-        def visit(h):
+    def spread(t, own, every, targets):
+        for h in targets:
             for o in mates:
                 a2a_copy(t, own, every, o, h).start()
-
-        in_order(visit)
 
     def fwd_copy(t, every, o, h, k):
         part = every.at[h, o, mine, :]
@@ -149,21 +145,28 @@
 
     def gather(t, every):
         out = {}
-        for o in (1, 2):
-            cp = remote(every.at[0], every.at[o], gat_s.at[t, o], gat_r.at[t, o], mate_id[o])
-            cp.start()
-            out[o] = cp
+        for u in (0, 1):
+            for o in (1, 2):
+                cp = remote(every.at[u, 0], every.at[u, o], gat_s.at[t, u, o], gat_r.at[t, u, o], mate_id[o])
+                cp.start()
+                out[u, o] = cp
         return out
 
-    def relay(t, every, copies):
+    def relay(t, u, every, copies):
         out = []
         for o, lo_row in ((1, 0), (2, half)):
-            copies[o].wait_recv()
+            copies[u, o].wait_recv()
             part = pl.ds(lo_row, half)
-            cp = remote(every.at[o, part], every.at[3, part], rel_s.at[t, o], rel_r.at[t, o], mate_id[3 - o])
+            cp = remote(
+                every.at[u, o, part], every.at[u, 3, part], rel_s.at[t, u, o], rel_r.at[t, u, o], mate_id[3 - o]
+            )
             cp.start()
             out.append(cp)
         return out
+
+    def turn(u, every, every_t, slots):
+        for o in slots:
+            every_t[u, :, o * rows:(o + 1) * rows] = every[u, o].T
 
     def to_owner(t, parts, got):
         out = []
@@ -174,19 +177,19 @@
             out.append(cp)
         return out
 
-    loads[1].wait()
+    loads[0].wait()
     loads[2].start()
-    loads[3].start()
-    mask_into(dy_raw, y_own)
+    mask_into(x_raw, x_own)
     pl.semaphore_wait(
         barrier,
         len(mate_id) + len(sib_id) + has_right.astype(jnp.int32) + has_left.astype(jnp.int32),
     )
 
-    spread(1, y_own, y_all)
-    loads[0].wait()
-    mask_into(x_raw, x_own)
     sib_x = share(0, x_own)
+    loads[1].wait()
+    loads[3].start()
+    mask_into(dy_raw, y_own)
+    spread(1, y_own, y_all, order[:-1])
     sib_y = share(1, y_own)
 
     loads[2].wait()
@@ -205,7 +208,9 @@
     def gelu_step(i, carry):
         r = pl.ds(pl.multiple_of(i * piece, piece), piece)
         value, sl = gelu_parts(pre[r, :])
-        h_all[0, r, :] = (value * gate).astype(BF16)
+        value = (value * gate).astype(BF16)
+        h_all[0, 0, r, :] = value[:, :wing]
+        h_all[1, 0, r, :] = value[:, wing:]
         slope[r, :] = sl
         return carry
 
@@ -224,38 +229,34 @@
                 y_own[l, h], wd[:, c * chunk:(c + 1) * chunk], nt, preferred_element_type=F32
             )
             acc = term if acc is None else acc + term
-    g_all[0] = (acc * slope[...]).astype(BF16) * gate.astype(BF16)
+    grad = (acc * slope[...]).astype(BF16) * gate.astype(BF16)
+    g_all[0, 0] = grad[:, :wing]
+    g_all[1, 0] = grad[:, wing:]
+    for u in (0, 1):
+        turn(u, h_all, h_t, (0,))
+    for h in range(steps):
+        y_all[h, 0] = y_own[lo, h]
+
+    rel_h = [relay(0, u, h_all, gat_h) for u in (0, 1)]
+    spread(1, y_own, y_all, order[-1:])
+    gat_g = gather(1, g_all)
+    turn(0, h_all, h_t, (1, 2))
 
     wide = 512
 
     def out_step(j, carry):
         cols = pl.ds(pl.multiple_of(j * wide, wide), wide)
-        out_part[:, cols] = jnp.dot(h_all[0], wd[:, cols], preferred_element_type=F32).astype(BF16)
+        total = jnp.dot(h_all[0, 0], wd[0:wing, cols], preferred_element_type=F32)
+        total = total + jnp.dot(h_all[1, 0], wd[wing:, cols], preferred_element_type=F32)
+        out_part[:, cols] = total.astype(BF16)
         return carry
-
-    lax.fori_loop(0, feats // wide, out_step, 0)
-    own_out = to_owner(0, out_part, out_got)
-    h_t[:, 0:rows] = h_all[0].T
-    for h in range(steps):
-        y_all[h, 0] = y_own[lo, h]
-
-    rel_h = relay(0, h_all, gat_h)
-    gat_g = gather(1, g_all)
 
     def in_step(j, carry):
         cols = pl.ds(pl.multiple_of(j * wide, wide), wide)
-        in_part[:, cols] = lax.dot_general(
-            g_all[0], wu[cols, :], nt, preferred_element_type=F32
-        ).astype(BF16)
+        total = lax.dot_general(g_all[0, 0], wu[cols, 0:wing], nt, preferred_element_type=F32)
+        total = total + lax.dot_general(g_all[1, 0], wu[cols, wing:], nt, preferred_element_type=F32)
+        in_part[:, cols] = total.astype(BF16)
         return carry
-
-    lax.fori_loop(0, feats // wide, in_step, 0)
-    own_in = to_owner(1, in_part, in_got)
-    g_t[:, 0:rows] = g_all[0].T
-    for h in range(steps):
-        x_all[h, 0] = x_own[lo, h]
-    for o in (1, 2):
-        h_t[:, o * rows:(o + 1) * rows] = h_all[o].T
 
     def finish(parts, got, raw, held, copies):
         for cp in copies:
@@ -271,26 +272,24 @@
 
         lax.fori_loop(0, feats // wide, step, 0)
 
-    finish(out_part, out_got, x_raw, mixed_v, own_out)
-    store_mixed = pltpu.make_async_copy(mixed_v, mixed_hbm, loc.at[4])
-    store_mixed.start()
-
-    def partial_of(t, h):
+    def partial_of(t, u, h):
         if t == 0:
             each_t, own, every = h_t, y_own, y_all
         else:
             each_t, own, every = g_t, x_own, x_all
-        forward(1 - t, own, every, h)
-        forwarded(1 - t, every, h)
-        return jnp.dot(each_t[...], every[h].reshape(GROUP * rows, chunk), preferred_element_type=F32)
-
-    def z_copy(t, side, d):
+        if u == 0:
+            forward(1 - t, own, every, h)
+            forwarded(1 - t, every, h)
+        return jnp.dot(each_t[u], every[h].reshape(GROUP * rows, chunk), preferred_element_type=F32)
+
+    def z_copy(q, side, d):
         return remote(
-            z_send.at[t, side, d - 1], z_got.at[t, side, d - 1], zs.at[t, side, d - 1], zr.at[t, side, d - 1],
+            z_send.at[q, side, d - 1], z_got.at[q, side, d - 1], zs.at[q, side, d - 1], zr.at[q, side, d - 1],
             side_id[side],
         )
 
-    def chain(t, between):
+    def chain(t, u, between):
+        q = 2 * t + u
         for d in range(steps - 1, 0, -1):
             if d == 1:
                 between()
@@ -299,58 +298,79 @@
 
                 @pl.when(sends)
                 def _():
-                    partial[t] = partial_of(t, hi + d if side == 0 else hi - d)
+                    partial[q] = partial_of(t, u, hi + d if side == 0 else hi - d)
                     if d < steps - 1:
                         @pl.when(behind)
                         def _():
-                            z_copy(t, side, d + 1).wait_recv()
-                            partial[t] = partial[t] + z_got[t, side, d].astype(F32)
-
-                    z_send[t, side, d - 1] = partial[t].astype(BF16)
-                    z_copy(t, side, d).start()
-
-        partial[t] = partial_of(t, hi)
-
-    def close(t):
+                            z_copy(q, side, d + 1).wait_recv()
+                            partial[q] = partial[q] + z_got[q, side, d].astype(F32)
+
+                    z_send[q, side, d - 1] = partial[q].astype(BF16)
+                    z_copy(q, side, d).start()
+
+        partial[q] = partial_of(t, u, hi)
+
+    def close(q):
         for side, behind in ((0, has_left), (1, has_right)):
             @pl.when(behind)
             def _():
-                z_copy(t, side, 1).wait_recv()
-                partial[t] = partial[t] + z_got[t, side, 0].astype(F32)
-
-        return partial[t] * inv
+                z_copy(q, side, 1).wait_recv()
+                partial[q] = partial[q] + z_got[q, side, 0].astype(F32)
+
+        return partial[q] * inv
+
+    def arrived(t, u, every, every_t, copies):
+        for cp in copies:
+            cp.wait_recv()
+        turn(u, every, every_t, (3,))
+
+    rel_g = []
 
     def pass_on():
-        rel_g.extend(relay(1, g_all, gat_g))
-        spread(0, x_own, x_all)
-
-    rel_g = []
-    for cp in rel_h:
-        cp.wait_recv()
-    h_t[:, 3 * rows:] = h_all[3].T
-    chain(0, pass_on)
-
-    for o in (1, 2):
-        g_t[:, o * rows:(o + 1) * rows] = g_all[o].T
+        for u in (0, 1):
+            rel_g.append(relay(1, u, g_all, gat_g))
+        spread(0, x_own, x_all, order)
+
+    def nothing():
+        pass
+
+    arrived(0, 0, h_all, h_t, rel_h[0])
+    chain(0, 0, nothing)
+    lax.fori_loop(0, feats // wide, out_step, 0)
+    own_out = to_owner(0, out_part, out_got)
+    turn(1, h_all, h_t, (1, 2))
+    for u in (0, 1):
+        turn(u, g_all, g_t, (0,))
+    for h in range(steps):
+        x_all[h, 0] = x_own[lo, h]
+    arrived(0, 1, h_all, h_t, rel_h[1])
+    chain(0, 1, pass_on)
+    lax.fori_loop(0, feats // wide, in_step, 0)
+    own_in = to_owner(1, in_part, in_got)
+    turn(0, g_all, g_t, (1, 2))
+    arrived(1, 0, g_all, g_t, rel_g[0])
+    chain(1, 0, nothing)
+    turn(1, g_all, g_t, (1, 2))
+    arrived(1, 1, g_all, g_t, rel_g[1])
+    finish(out_part, out_got, x_raw, mixed_v, own_out)
+    store_mixed = pltpu.make_async_copy(mixed_v, mixed_hbm, loc.at[4])
+    store_mixed.start()
+    chain(1, 1, nothing)
     finish(in_part, in_got, dy_raw, ing_v, own_in)
     store_ing = pltpu.make_async_copy(ing_v, ing_hbm, loc.at[5])
     store_ing.start()
 
-    for cp in rel_g:
-        cp.wait_recv()
-    g_t[:, 3 * rows:] = g_all[3].T
-    chain(1, lambda: None)
-
-    grad_v[...] = close(0)
+    grad_v[0:wing] = close(0)
+    grad_v[wing:] = close(1)
     store_down = pltpu.make_async_copy(grad_v, down_hbm, loc.at[6])
     store_down.start()
-    pre_t = close(1)
     up_v = pre.at[0:chunk, :]
-    up_v[...] = pre_t.T
+    pre[0:chunk, 0:wing] = close(2).T
+    pre[0:chunk, wing:] = close(3).T
     store_up = pltpu.make_async_copy(up_v, up_hbm, loc.at[7])
     store_up.start()
 
-    for cp in sib_x + sib_y + own_out + own_in + rel_h + rel_g:
+    for cp in sib_x + sib_y + own_out + own_in + sum(rel_h + rel_g, []):
         cp.wait_send()
 
     def drain(h, carry):
@@ -365,29 +385,32 @@
     for group in (gat_h, gat_g):
         for cp in group.values():
             cp.wait_send()
-    for t in (0, 1):
+    for q in range(4):
         for d in range(steps - 1, 0, -1):
             for side in (0, 1):
                 sends, _ = z_conditions(side, d)
 
                 @pl.when(sends)
                 def _():
-                    z_copy(t, side, d).wait_send()
+                    z_copy(q, side, d).wait_send()
     for cp in (store_mixed, store_ing, store_down, store_up):
         cp.wait()
 
 
 def hand_over(*refs):
-    copies = []
-    sems = refs[-1]
+    held, sems = refs[8:12], refs[12]
+    parts = []
     for i in range(4):
         size = refs[i].shape[1] // 2
-        for j in range(2):
-            part = pl.ds(j * size, size)
-            copies.append(pltpu.make_async_copy(refs[i].at[:, part], refs[4 + i].at[:, part], sems.at[i, j]))
-    for cp in copies:
+        parts += [(i, j, pl.ds(j * size, size)) for j in range(2)]
+    reads = [pltpu.make_async_copy(refs[i].at[:, p], held[i].at[:, p], sems.at[0, i, j]) for i, j, p in parts]
+    writes = [pltpu.make_async_copy(held[i].at[:, p], refs[4 + i].at[:, p], sems.at[1, i, j]) for i, j, p in parts]
+    for cp in reads:
         cp.start()
-    for cp in copies:
+    for get, put in zip(reads, writes):
+        get.wait()
+        put.start()
+    for cp in writes:
         cp.wait()
 
 
@@ -410,19 +433,19 @@
         pltpu.VMEM((GROUP, steps, rows, chunk), BF16),
         pltpu.VMEM((steps, GROUP, rows, chunk), BF16),
         pltpu.VMEM((steps, GROUP, rows, chunk), BF16),
-        pltpu.VMEM((GROUP, rows, units), BF16),
-        pltpu.VMEM((GROUP, rows, units), BF16),
-        pltpu.VMEM((units, GROUP * rows), BF16),
-        pltpu.VMEM((units, GROUP * rows), BF16),
+        pltpu.VMEM((2, GROUP, rows, units // 2), BF16),
+        pltpu.VMEM((2, GROUP, rows, units // 2), BF16),
+        pltpu.VMEM((2, units // 2, GROUP * rows), BF16),
+        pltpu.VMEM((2, units // 2, GROUP * rows), BF16),
         pltpu.VMEM((rows, units), F32),
         pltpu.VMEM((rows, units), F32),
         pltpu.VMEM((rows, feats), BF16),
         pltpu.VMEM((rows, feats), BF16),
         pltpu.VMEM((n_blk - 1, rows_own, feats), BF16),
         pltpu.VMEM((n_blk - 1, rows_own, feats), BF16),
-        pltpu.VMEM((2, units, chunk), F32),
-        pltpu.VMEM((2, 2, hops, units, chunk), BF16),
-        pltpu.VMEM((2, 2, hops, units, chunk), BF16),
+        pltpu.VMEM((4, units // 2, chunk), F32),
+        pltpu.VMEM((4, 2, hops, units // 2, chunk), BF16),
+        pltpu.VMEM((4, 2, hops, units // 2, chunk), BF16),
         pltpu.VMEM((rows_own, feats), BF16),
         pltpu.VMEM((rows_own, feats), BF16),
         pltpu.VMEM((units, chunk), F32),
@@ -430,10 +453,10 @@
         dma((2, n_blk)), dma((2, n_blk)),
         dma((2, GROUP, steps)), dma((2, GROUP, steps)),
         dma((2, GROUP, steps, n_blk)), dma((2, GROUP, steps, n_blk)),
-        dma((2, GROUP)), dma((2, GROUP)),
-        dma((2, GROUP)), dma((2, GROUP)),
+        dma((2, 2, GROUP)), dma((2, 2, GROUP)),
+        dma((2, 2, GROUP)), dma((2, 2, GROUP)),
         dma((2, n_blk)), dma((2, n_blk)),
-        dma((2, 2, hops)), dma((2, 2, hops)),
+        dma((4, 2, hops)), dma((4, 2, hops)),
     ]
     mixed, ing, up, down = pl.pallas_call(
         functools.partial(kernel, n_dp, n_blk),
@@ -459,7 +482,8 @@
         out_shape=tuple(jax.ShapeDtypeStruct(r.shape, r.dtype) for r in results),
         in_specs=[anywhere] * 4,
         out_specs=(anywhere,) * 4,
-        scratch_shapes=[dma((4, 2))],
+        scratch_shapes=[pltpu.VMEM(r.shape, r.dtype) for r in results] + [dma((2, 4, 2))],
+        compiler_params=pltpu.CompilerParams(vmem_limit_bytes=16 * 1024 * 1024),
     )(*results)
 
 

time: 171 us -> 80.3 us (0.47)
  Pallas kernels: 170 us -> 74.8 us
  local copies, waits for them, and re-layouts: 0 us -> 4.52 us
    pallas_call x1, Pallas kernels: 96.5 us -> 2 us  [local(): pl.pallas_call(hand_over, out_shape=tuple((jax.ShapeDtypeStruct(r.shape,...]
    unnamed x0 -> x8, local copies, waits for them, and re-layouts: none -> 4.52 us
where the time goes in v3:
time: 80.3 us; the launch traced here: 80 us
  Pallas kernels  74.8 us (93%)
  local copies, waits for them, and re-layouts  4.52 us (6%)
    pallas_call x1, Pallas kernels, local(): pl.pallas_call(functools.partial(kernel, n_dp, n_blk), out_shape=(jax.Sha...  72.8 us
    unnamed x8, local copies, waits for them, and re-layouts  4.52 us
    pallas_call x1, Pallas kernels, local(): pl.pallas_call(hand_over, out_shape=tuple((jax.ShapeDtypeStruct(r.shape,...  2 us

profile of v3, /device:TPU:0, one launch (start us, length us, event | category | flops | bytes accessed | tf_op | source)
XLA Modules:
  0.0 80.0 jit_solution(15730152282236107801)
XLA Ops:
  0.6 72.8 %shard_map.102 = (bf16[128,4096]{1,0:T(8,128)(2,1)}, bf16[128,4096]{1,0:T(8,128)(2,1)}, f32[256,512]{1,0:T(8,128)}, f32[512,256]{1,0:T(8,128)}) custom-call(bf16[128,4096]{1,0:T(8,128)(2,1)} %bitcast.15, bf16[128,4096]{1,0:T(8,128)(2,1)} %bitcast.16, bf16[4096,512]{1,0:T(8,128)(2,1)} %bitcast.13, bf16[512,4096]{1,0:T(8,128)(2,1)} %bitcast.14, ...), custom_call_target="tpu_custom_call" | custom-call | flops 6442450944 | bytes 16777216 | tf_op jit(solution)/shard_map/pallas_call | solution.py:461
  73.4 0.0 copy-start
  73.4 1.2 %copy-done = bf16[128,4096]{1,0:T(8,128)(2,1)S(1)} copy-done((bf16[128,4096]{1,0:T(8,128)(2,1)S(1)}, bf16[128,4096]{1,0:T(8,128)(2,1)}, u32[]{:S(2)}) %copy-start) | copy-done | bytes 1048600
  74.7 0.0 copy-start.1
  74.7 1.2 %copy-done.1 = bf16[128,4096]{1,0:T(8,128)(2,1)S(1)} copy-done((bf16[128,4096]{1,0:T(8,128)(2,1)S(1)}, bf16[128,4096]{1,0:T(8,128)(2,1)}, u32[]{:S(2)}) %copy-start.1) | copy-done | bytes 1048600
  75.9 0.0 copy-start.2
  75.9 1.0 %copy-done.2 = f32[256,512]{1,0:T(8,128)S(1)} copy-done((f32[256,512]{1,0:T(8,128)S(1)}, f32[256,512]{1,0:T(8,128)}, u32[]{:S(2)}) %copy-start.2) | copy-done | bytes 524312
  76.9 0.0 copy-start.3
  76.9 1.0 %copy-done.3 = f32[512,256]{1,0:T(8,128)S(1)} copy-done((f32[512,256]{1,0:T(8,128)S(1)}, f32[512,256]{1,0:T(8,128)}, u32[]{:S(2)}) %copy-start.3) | copy-done | bytes 524312
  78.0 2.0 %shard_map.103 = (bf16[1,128,4096]{2,1,0:T(8,128)(2,1)}, bf16[1,128,4096]{2,1,0:T(8,128)(2,1)}, f32[1,256,512]{2,1,0:T(8,128)}, f32[1,512,256]{2,1,0:T(8,128)}) custom-call(bf16[1,128,4096]{2,1,0:T(8,128)(2,1)S(1)} %bitcast.9, bf16[1,128,4096]{2,1,0:T(8,128)(2,1)S(1)} %bitcast.10, f32[1,256,512]{2,1,0:T(8,128)S(1)} %bitcast.11, f32[1,512,256]{2,1,0:T(8,128)S(1)} %bitcast.12), custom_call_target="tpu_custom_call" | custom-call | tf_op jit(solution)/shard_map/pallas_call | solution.py:480
Async XLA Ops:
  73.4 1.2 %copy-start = (bf16[128,4096]{1,0:T(8,128)(2,1)S(1)}, bf16[128,4096]{1,0:T(8,128)(2,1)}, u32[]{:S(2)}) copy-start(bf16[128,4096]{1,0:T(8,128)(2,1)} %get-tuple-element.8) | copy-start | bytes 3145732
  74.7 1.2 %copy-start.1 = (bf16[128,4096]{1,0:T(8,128)(2,1)S(1)}, bf16[128,4096]{1,0:T(8,128)(2,1)}, u32[]{:S(2)}) copy-start(bf16[128,4096]{1,0:T(8,128)(2,1)} %get-tuple-element.9) | copy-start | bytes 3145732
  75.9 1.0 %copy-start.2 = (f32[256,512]{1,0:T(8,128)S(1)}, f32[256,512]{1,0:T(8,128)}, u32[]{:S(2)}) copy-start(f32[256,512]{1,0:T(8,128)} %get-tuple-element.10) | copy-start | bytes 1572868
  76.9 1.0 %copy-start.3 = (f32[512,256]{1,0:T(8,128)S(1)}, f32[512,256]{1,0:T(8,128)}, u32[]{:S(2)}) copy-start(f32[512,256]{1,0:T(8,128)} %get-tuple-element.11) | copy-start | bytes 1572868

commit v4 on v3

--- a/solution.py
+++ b/solution.py
@@ -483,7 +483,7 @@
         in_specs=[anywhere] * 4,
         out_specs=(anywhere,) * 4,
         scratch_shapes=[pltpu.VMEM(r.shape, r.dtype) for r in results] + [dma((2, 4, 2))],
-        compiler_params=pltpu.CompilerParams(vmem_limit_bytes=16 * 1024 * 1024),
+        compiler_params=pltpu.CompilerParams(vmem_limit_bytes=60 * 1024 * 1024),
     )(*results)
 
 

time: 80.3 us -> 76.4 us (0.951)
  local copies, waits for them, and re-layouts: 4.52 us -> 0 us
    unnamed x8 -> x0, local copies, waits for them, and re-layouts: 4.52 us -> none
    pallas_call x1, Pallas kernels: 2 us -> 2.83 us  [local(): pl.pallas_call(hand_over, out_shape=tuple((jax.ShapeDtypeStruct(r.shape,...]
where the time goes in v4:
time: 76.4 us; the launch traced here: 76.3 us
  Pallas kernels  75.6 us (99%)
    pallas_call x1, Pallas kernels, local(): pl.pallas_call(functools.partial(kernel, n_dp, n_blk), out_shape=(jax.Sha...  72.8 us
    pallas_call x1, Pallas kernels, local(): pl.pallas_call(hand_over, out_shape=tuple((jax.ShapeDtypeStruct(r.shape,...  2.83 us

profile of v4, /device:TPU:0, one launch (start us, length us, event | category | flops | bytes accessed | tf_op | source)
XLA Modules:
  0.0 76.3 jit_solution(17582975790640352186)
XLA Ops:
  0.6 72.8 %shard_map.102 = (bf16[128,4096]{1,0:T(8,128)(2,1)}, bf16[128,4096]{1,0:T(8,128)(2,1)}, f32[256,512]{1,0:T(8,128)}, f32[512,256]{1,0:T(8,128)}) custom-call(bf16[128,4096]{1,0:T(8,128)(2,1)} %bitcast.15, bf16[128,4096]{1,0:T(8,128)(2,1)} %bitcast.16, bf16[4096,512]{1,0:T(8,128)(2,1)} %bitcast.13, bf16[512,4096]{1,0:T(8,128)(2,1)} %bitcast.14, ...), custom_call_target="tpu_custom_call" | custom-call | flops 6442450944 | bytes 16777216 | tf_op jit(solution)/shard_map/pallas_call | solution.py:461
  73.4 2.8 %shard_map.103 = (bf16[1,128,4096]{2,1,0:T(8,128)(2,1)}, bf16[1,128,4096]{2,1,0:T(8,128)(2,1)}, f32[1,256,512]{2,1,0:T(8,128)}, f32[1,512,256]{2,1,0:T(8,128)}) custom-call(bf16[1,128,4096]{2,1,0:T(8,128)(2,1)} %bitcast.9, bf16[1,128,4096]{2,1,0:T(8,128)(2,1)} %bitcast.10, f32[1,256,512]{2,1,0:T(8,128)} %bitcast.11, f32[1,512,256]{2,1,0:T(8,128)} %bitcast.12), custom_call_target="tpu_custom_call" | custom-call | tf_op jit(solution)/shard_map/pallas_call | solution.py:480
